TPU v7x, 32 devices: a whole 2x2x4 slice. The times are simulated.
32 devices in a mesh: groups: 2 (over x), ctx: 16 (over z, y, core).
Axes of the slice: x: 2, y: 2, z: 4, core: 2. Of those that a mesh axis runs over, the one named last changes fastest.
Arguments:
- queries: bfloat16 [128, 4096], P(('groups', 'ctx')), parts along dimension 0, may hold values from -110 to 110
- keys: bfloat16 [16, 65536, 128], P(None, ('groups', 'ctx')), parts along dimension 1, may hold values from -8 to 8
- values: bfloat16 [16, 65536, 128], P(None, ('groups', 'ctx')), parts along dimension 1, may hold values from -6 to 6
- residual: bfloat16 [128, 5376], P(('groups', 'ctx')), parts along dimension 0, may hold values from -6 to 6
- post_gain: float32 [5376], replicated, may hold values from 0.5 to 1.5
- out_weight: bfloat16 [4096, 5376], P('ctx'), may hold values from -0.09375 to 0.09375
Outputs:
- updated: float32 [128, 5376], P(('groups', 'ctx')), parts along dimension 0
There are 2 independent parts, one for each index of `groups`. A program takes and returns all parts, laid end to end along the dimension named above; an argument that names none is the same for every part. Nothing has to cross between parts.
All inputs are finite; a program needn't handle non-finite values.
Results may differ from a plain program's by a relative error of at most 0.017.
Values may be sent and summed in bfloat16 or wider, within the bound.
A program may use at most 320 MiB of HBM per device.

v0:
```python
import jax
import jax.numpy as jnp
from jax import lax
from jax.sharding import PartitionSpec as P

query_scale = 168.0 ** (-0.5)


def partial_head(operands):
    head_queries, head_keys, head_values = operands
    scores = (
        lax.dot_general(
            head_queries, head_keys, (((1,), (1,)), ((), ())), preferred_element_type=jnp.float32
        )
        * query_scale
    )
    row_max = jnp.max(scores, axis=1)
    exponent = jnp.exp(scores - row_max[:, None])
    row_total = jnp.sum(exponent, axis=1)
    weights = exponent.astype(jnp.bfloat16)
    weighted = jnp.dot(weights, head_values, preferred_element_type=jnp.float32)
    return (row_max, row_total, weighted)


def shards(queries, keys, values, residual, post_gain, out_weight):
    all_queries = lax.all_gather(queries, "ctx", axis=0, tiled=True)
    kv_heads = keys.shape[0]
    head_dim = keys.shape[2]
    unit_count = all_queries.shape[0]
    head_count = all_queries.shape[1] // head_dim
    group_size = head_count // kv_heads
    grouped = (
        all_queries.reshape(unit_count, kv_heads, group_size, head_dim)
        .transpose(1, 0, 2, 3)
        .reshape(kv_heads, unit_count * group_size, head_dim)
    )
    row_max, row_total, weighted = lax.map(partial_head, (grouped, keys, values))
    row_max = (
        row_max.reshape(kv_heads, unit_count, group_size)
        .transpose(1, 0, 2)
        .reshape(unit_count, head_count)
    )
    row_total = (
        row_total.reshape(kv_heads, unit_count, group_size)
        .transpose(1, 0, 2)
        .reshape(unit_count, head_count)
    )
    weighted = (
        weighted.reshape(kv_heads, unit_count, group_size, head_dim)
        .transpose(1, 0, 2, 3)
        .reshape(unit_count, head_count * head_dim)
    )
    own_width = out_weight.shape[0]
    peak_parts, total_parts, weighted_parts = (
        lax.all_to_all(row_max[None], "ctx", split_axis=2, concat_axis=0, tiled=True),
        lax.all_to_all(row_total[None], "ctx", split_axis=2, concat_axis=0, tiled=True),
        lax.all_to_all(weighted[None], "ctx", split_axis=2, concat_axis=0, tiled=True),
    )
    own_heads = own_width // head_dim
    overall = jnp.max(peak_parts, axis=0)
    factor = jnp.exp(peak_parts - overall[None])
    summed_total = jnp.sum(total_parts * factor, axis=0)
    summed = jnp.sum(
        weighted_parts.reshape(-1, unit_count, own_heads, head_dim) * factor[:, :, :, None], axis=0
    )
    own_block = (
        (summed / summed_total[:, :, None]).reshape(unit_count, own_width).astype(jnp.bfloat16)
    )
    branch = lax.psum_scatter(
        jnp.dot(own_block, out_weight, preferred_element_type=jnp.float32).astype(jnp.bfloat16),
        "ctx",
        scatter_dimension=0,
        tiled=True,
    ).astype(jnp.float32)
    mean_square = jnp.mean(branch * branch, axis=1, keepdims=True)
    normed = branch * lax.rsqrt(mean_square + 1e-06) * post_gain
    return residual.astype(jnp.float32) + normed


def solution(mesh):
    in_specs = (
        P(("groups", "ctx"), None),
        P(None, ("groups", "ctx"), None),
        P(None, ("groups", "ctx"), None),
        P(("groups", "ctx"), None),
        P(),
        P("ctx", None),
    )
    out_specs = P(("groups", "ctx"), None)
    return jax.shard_map(shards, mesh=mesh, in_specs=in_specs, out_specs=out_specs, check_vma=False)
```

profile of v0, /device:TPU:0, one launch (start us, length us, event | category | flops | bytes accessed | tf_op | source)
XLA Modules:
  0.0 324.7 jit_solution(10710078126113565020)
XLA Ops:
  6.5 26.5 %all-gather = bf16[16,4,4096]{2,1,0:T(4,128)(2,1)} all-gather(bf16[1,4,4096]{2,1,0:T(4,128)(2,1)} %bitcast.95), channel_id=1, replica_groups=mesh['groups'=2,'ctx'=16] {'ctx'}, dimensions={0}, use_global_device_ids=true | all-gather | bytes 557056 | tf_op jit(solution)/shard_map/all_gather | solution.py:26
  35.9 100.3 %while.14 = (s32[]{:T(128)}, f32[16,128]{1,0:T(8,128)S(1)}, f32[16,128]{1,0:T(8,128)S(1)}, f32[16,128,128]{2,1,0:T(8,128)}, bf16[16,128,128]{2,1,0:T(8,128)(2,1)...) while((s32[]{:T(128)}, f32[16,128]{1,0:T(8,128)S(1)}, ...), condition=%wide.region_3.4_spmd, body=%wide.region_0.3_spmd.sunk | while | flops 135790336 | bytes 4298861 | solution.py:37
  35.9 2.4 fusion.28
  42.2 2.4 fusion.28
  54.8 2.4 fusion.28
  61.0 2.4 fusion.28
  79.8 2.4 fusion.28
  86.1 2.4 fusion.28
  92.4 2.4 fusion.28
  108.9 2.4 fusion.30
  111.2 2.4 fusion.28
  117.5 2.4 fusion.28
  130.0 2.4 fusion.28
  138.3 3.5 %all-to-all-start.2 = ((f32[16,1,128]{2,1,0:T(1,128)}), f32[16,1,128]{2,1,0:T(1,128)S(1)}, u32[]{:S(2)}, u32[]{:S(2)}) async-start(f32[16,1,128]{2,1,0:T(1,128)} %reshape.56), calls=%async_computation.2 | async-start | bytes 16384 | tf_op jit(solution)/shard_map/all_to_all | solution.py:56
  143.3 4.8 %all-to-all-done.2 = f32[16,1,128]{2,1,0:T(1,128)S(1)} async-done(((f32[16,1,128]{2,1,0:T(1,128)}), f32[16,1,128]{2,1,0:T(1,128)S(1)}, u32[]{:S(2)}, u32[]{:S(2)}) %all-to-all-start.2) | async-done | bytes 8224 | tf_op jit(solution)/shard_map/all_to_all | solution.py:56
  148.1 3.4 %all-to-all-start.1 = ((f32[16,1,128]{2,1,0:T(1,128)}), f32[16,1,128]{2,1,0:T(1,128)S(1)}, u32[]{:S(2)}, u32[]{:S(2)}) async-start(f32[16,1,128]{2,1,0:T(1,128)} %reshape.54), calls=%async_computation.1 | async-start | bytes 16384 | tf_op jit(solution)/shard_map/all_to_all | solution.py:55
  151.5 2.8 copy.34
  154.3 20.3 %reduce.2 = f32[4096,64]{1,0:T(8,128)} reduce(f32[4096,1,64]{2,1,0:T(1,128)} %bitcast.82, f32[]{:T(128)} %broadcast.40), dimensions={1}, to_apply=%bitcast.57.reduce_sub_computation | reduce | bytes 2097156
  174.6 3.4 %reshape.52 = f32[16,1,16384]{2,1,0:T(1,128)} reshape(f32[4096,64]{1,0:T(8,128)} %reduce.2) | data formatting | bytes 2097152
  178.1 6.0 %all-to-all-start = ((f32[16,1,16384]{2,1,0:T(1,128)}), f32[16,1,16384]{2,1,0:T(1,128)}, u32[]{:S(2)}, u32[]{:S(2)}) async-start(f32[16,1,16384]{2,1,0:T(1,128)} %reshape.52), calls=%async_computation | async-start | bytes 2097152 | tf_op jit(solution)/shard_map/all_to_all | solution.py:57
  185.8 21.3 %all-to-all-done = f32[16,1,16384]{2,1,0:T(1,128)} async-done(((f32[16,1,16384]{2,1,0:T(1,128)}), f32[16,1,16384]{2,1,0:T(1,128)}, u32[]{:S(2)}, u32[]{:S(2)}) %all-to-all-start) | async-done | bytes 1048608 | tf_op jit(solution)/shard_map/all_to_all | solution.py:57
  207.1 5.3 %reduce.3 = f32[16,16384]{1,0:T(8,128)} reduce(f32[16,1,16384]{2,1,0:T(1,128)} %all-to-all-done, f32[]{:T(128)} %broadcast.40), dimensions={1}, to_apply=%all_to_all.37.reduce_sub_computation | reduce | bytes 2097156 | tf_op jit(solution)/shard_map/all_to_all | solution.py:57
  212.4 5.2 %reshape.53 = f32[4096,1,64]{2,1,0:T(1,128)} reshape(f32[16,16384]{1,0:T(8,128)} %reduce.3) | data formatting | bytes 2097152
  222.3 92.9 %all-reduce.3.cloned.1.call-done = bf16[64,5376]{1,0:T(8,128)(2,1)} async-done(((bf16[64,5376]{1,0:T(8,128)(2,1)}), bf16[64,5376]{1,0:T(8,128)(2,1)}) %all-reduce.3.cloned.1.call-update) | async-done | bytes 688144
  (107 shorter events, 89.2 us)
Async XLA Ops:
  6.5 213.0 %copy-start = (bf16[256,5376]{1,0:T(8,128)(2,1)S(1)}, bf16[256,5376]{1,0:T(8,128)(2,1)}, u32[]{:S(2)}) copy-start(bf16[256,5376]{1,0:T(8,128)(2,1)} %param.13) | copy-start | bytes 8257540
  138.3 9.8 %all-to-all-start.2 = ((f32[16,1,128]{2,1,0:T(1,128)}), f32[16,1,128]{2,1,0:T(1,128)S(1)}, u32[]{:S(2)}, u32[]{:S(2)}) async-start(f32[16,1,128]{2,1,0:T(1,128)} %reshape.56), calls=%async_computation.2 | async-start | bytes 16384 | tf_op jit(solution)/shard_map/all_to_all | solution.py:56
  148.1 29.9 %all-to-all-start.1 = ((f32[16,1,128]{2,1,0:T(1,128)}), f32[16,1,128]{2,1,0:T(1,128)S(1)}, u32[]{:S(2)}, u32[]{:S(2)}) async-start(f32[16,1,128]{2,1,0:T(1,128)} %reshape.54), calls=%async_computation.1 | async-start | bytes 16384 | tf_op jit(solution)/shard_map/all_to_all | solution.py:55
  178.1 29.0 %all-to-all-start = ((f32[16,1,16384]{2,1,0:T(1,128)}), f32[16,1,16384]{2,1,0:T(1,128)}, u32[]{:S(2)}, u32[]{:S(2)}) async-start(f32[16,1,16384]{2,1,0:T(1,128)} %reshape.52), calls=%async_computation | async-start | bytes 2097152 | tf_op jit(solution)/shard_map/all_to_all | solution.py:57
  184.1 131.1 %all-reduce.3.cloned.1.call-start = ((), (), s32[]{:S(2)}) async-start(), calls=%async_computation.3 | async-start | bytes 1376256
  219.4 1.6 copy-start.3
  219.5 96.8 %copy-start.1 = (bf16[4,5376]{1,0:T(4,128)(2,1)S(1)}, bf16[4,5376]{1,0:T(4,128)(2,1)}, u32[]{:S(2)}) copy-start(bf16[4,5376]{1,0:T(4,128)(2,1)} %param.11) | copy-start | bytes 129028
  219.5 96.8 %copy-start.2 = (f32[5376]{0:T(1024)S(1)}, f32[5376]{0:T(1024)}, u32[]{:S(2)}) copy-start(f32[5376]{0:T(1024)} %param.12) | copy-start | bytes 64516
Sparse Core Ops, SparseCore 0:
  221.2 93.9 all-reduce.2
where the time goes:
time: 327 us; the launch traced here: 325 us
  waiting for transfers between devices  119 us (36%)
  matrix products  76.6 us (23%)
  other arithmetic  57 us (17%)
  blocking collectives  26.5 us (8%)
  local copies, waits for them, and re-layouts  18.3 us (6%)
  between operations  14.2 us (4%)
  starting transfers between devices  13.1 us (4%)
    unnamed x2, waiting for transfers between devices  92.9 us
    dot_general x16, matrix products, partial_head(): lax.dot_general(head_queries, head_keys, (((1,), (1,)), ((), ())), prefer...  37.7 us
    dot_general x16, matrix products, partial_head(): weighted = jnp.dot(weights, head_values, preferred_element_type=jnp.float32)  37.4 us
    all_gather x1, blocking collectives, shards(): all_queries = lax.all_gather(queries, 'ctx', axis=0, tiled=True)  26.5 us
    reduce_sum x16, other arithmetic, partial_head(): row_total = jnp.sum(exponent, axis=1)  24.2 us
    unnamed x3, other arithmetic  21.6 us
    all_to_all x1, waiting for transfers between devices, shards(): lax.all_to_all(weighted[None], 'ctx', split_axis=2, concat_axis=0, tiled=...  21.3 us
    unnamed x16, local copies, waits for them, and re-layouts  11.3 us
  transfers between devices with their start and end apart: 4, of which 3 were waited for; matrix products, arithmetic and copies ran while one was open for 9% of the time, Pallas kernels for 0%

commit v1 on v0

v1 whole, which is shorter than its diff:
```python
import functools
import math

import jax
import jax.numpy as jnp
from jax import lax
from jax.experimental import pallas as pl
from jax.experimental.pallas import tpu as pltpu
from jax.sharding import PartitionSpec as P

MESH = pl.DeviceIdType.MESH
f32, bf16 = jnp.float32, jnp.bfloat16


def chunk_of(extent, largest):
    return max(c for c in range(128, largest + 1, 128) if extent % c == 0)


def kernel(
    n,
    group_size,
    q_ref,
    k_hbm,
    v_hbm,
    res_ref,
    gain_ref,
    w_hbm,
    out_ref,
    k_buf,
    v_buf,
    w_buf,
    q_all,
    part_out,
    stat_out,
    part_in,
    stat_in,
    y_out,
    y_in,
    k_sem,
    v_sem,
    w_sem,
    q_send,
    q_recv,
    p_send,
    p_recv,
    s_send,
    s_recv,
    y_send,
    y_recv,
):
    me = lax.axis_index("ctx")
    core = lax.rem(me, 2)
    sibling = me + 1 - 2 * core
    kv_heads, context, head_dim = k_buf.shape
    own_units = q_ref.shape[0]
    owners = n // kv_heads
    own_heads = group_size // owners
    own_rows = own_units * group_size
    rows = n * own_rows
    units = n * own_units
    width = w_buf.shape[1]
    scale = 168.0**-0.5 * math.log2(math.e)
    own_head = lax.div(me, owners)

    def head_at(step):
        return lax.rem(own_head + 1 + step, kv_heads)

    def k_copy(h):
        return pltpu.make_async_copy(k_hbm.at[h], k_buf.at[h], k_sem.at[h])

    def v_copy(h):
        return pltpu.make_async_copy(v_hbm.at[h], v_buf.at[h], v_sem.at[h])

    w_copy = pltpu.make_async_copy(w_hbm, w_buf, w_sem)

    @pl.loop(0, kv_heads)
    def _(step):
        k_copy(head_at(step)).start()
        v_copy(head_at(step)).start()

    w_copy.start()

    barrier = pltpu.get_barrier_semaphore()

    @pl.loop(1, n)
    def _(step):
        pl.semaphore_signal(
            barrier, inc=1, device_id={"ctx": lax.rem(me + step, n)}, device_id_type=MESH
        )

    own = q_ref[...].astype(f32)
    for h in range(kv_heads):
        first = h * group_size * head_dim
        q_all[me, h] = jnp.concatenate(
            [own[:, first + g * head_dim :][:, :head_dim] for g in range(group_size)], axis=0
        ).astype(bf16)

    pl.semaphore_wait(barrier, n - 1)

    def q_copy(block, target, slot):
        return pltpu.make_async_remote_copy(
            src_ref=q_all.at[block],
            dst_ref=q_all.at[block],
            send_sem=q_send.at[slot],
            recv_sem=q_recv.at[block],
            device_id={"ctx": target},
            device_id_type=MESH,
        )

    half = n // 2

    def peer(step):
        return lax.rem(me + 2 * step, n)

    @pl.loop(1, half)
    def _(step):
        q_copy(me, peer(step), step).start()

    q_copy(me, sibling, 0).start()

    @pl.loop(1, half)
    def _(step):
        source = peer(half - step)
        q_copy(source, sibling, 0).wait_recv()
        q_copy(source, sibling, half + step).start()

    @pl.loop(0, half)
    def _(step):
        q_copy(lax.rem(sibling + 2 * step, n), sibling, 0).wait_recv()

    def part_copy(h, p, source):
        slot = h * owners + p
        return (
            pltpu.make_async_remote_copy(
                src_ref=part_out.at[h],
                dst_ref=part_in.at[source],
                send_sem=p_send.at[slot],
                recv_sem=p_recv.at[source],
                device_id={"ctx": slot},
                device_id_type=MESH,
            ),
            pltpu.make_async_remote_copy(
                src_ref=stat_out.at[h],
                dst_ref=stat_in.at[source],
                send_sem=s_send.at[slot],
                recv_sem=s_recv.at[source],
                device_id={"ctx": slot},
                device_id_type=MESH,
            ),
        )

    tile = chunk_of(context, 512)

    @pl.loop(0, kv_heads)
    def _(step):
        h = head_at(step)
        q = q_all[:, h].astype(f32).reshape(rows, head_dim).astype(bf16)
        k_copy(h).wait()
        scores = [
            lax.dot_general(
                k_buf[h, pl.ds(t, tile), :],
                q,
                (((1,), (1,)), ((), ())),
                preferred_element_type=f32,
            )
            for t in range(0, context, tile)
        ]
        peak = functools.reduce(
            jnp.maximum, [jnp.max(s, axis=0, keepdims=True) for s in scores]
        ) * scale
        v_copy(h).wait()
        total = jnp.zeros((1, rows), f32)
        weighted = jnp.zeros((head_dim, rows), f32)
        for i, s in enumerate(scores):
            exponent = jnp.exp2(s * scale - peak)
            total += jnp.sum(exponent, axis=0, keepdims=True)
            weighted += lax.dot_general(
                v_buf[h, pl.ds(i * tile, tile), :],
                exponent.astype(bf16),
                (((0,), (0,)), ((), ())),
                preferred_element_type=f32,
            )
        row = lax.broadcasted_iota(jnp.int32, (8, rows), 0)
        part_out[h] = weighted.astype(bf16)
        stat_out[h] = jnp.where(row == 0, peak, total)
        for p in range(owners):

            @pl.when(h * owners + p != me)
            def _():
                for copy in part_copy(h, p, me):
                    copy.start()

    part_in[me] = part_out[own_head]
    stat_in[me] = stat_out[own_head]

    @pl.loop(1, n)
    def _(step):
        for copy in part_copy(0, 0, lax.rem(me + step, n)):
            copy.wait_recv()

    stats = stat_in[...]
    overall = jnp.max(stats, axis=0)[0:1, :]
    total = jnp.zeros((1, rows), f32)
    weighted = jnp.zeros((head_dim, rows), f32)
    for k in range(n):
        factor = jnp.exp2(stats[k, 0:1, :] - overall)
        total += factor * stats[k, 1:2, :]
        weighted += factor * part_in[k].astype(f32)
    attended = (weighted / total).astype(bf16)

    unit = lax.broadcasted_iota(jnp.int32, (units, rows), 0)
    column = lax.broadcasted_iota(jnp.int32, (units, rows), 1)
    first = lax.rem(me, owners) * own_heads
    blocks = []
    for g in range(own_heads):
        place = (
            lax.div(unit, own_units) * own_rows + (first + g) * own_units + lax.rem(unit, own_units)
        )
        pick = jnp.where(column == place, 1.0, 0.0).astype(bf16)
        blocks.append(
            lax.dot_general(
                pick, attended, (((1,), (1,)), ((), ())), preferred_element_type=f32
            ).astype(bf16)
        )
    own_block = jnp.concatenate(blocks, axis=1) if own_heads > 1 else blocks[0]

    w_copy.wait()
    step_width = chunk_of(width, 1024)
    for c in range(0, width, step_width):
        y = jnp.dot(own_block, w_buf[:, c : c + step_width], preferred_element_type=f32)
        for k in range(n):
            y_out[k, :, c : c + step_width] = y[k * own_units : (k + 1) * own_units].astype(bf16)

    def y_copy(target, source):
        return pltpu.make_async_remote_copy(
            src_ref=y_out.at[target],
            dst_ref=y_in.at[source],
            send_sem=y_send.at[target],
            recv_sem=y_recv.at[source],
            device_id={"ctx": target},
            device_id_type=MESH,
        )

    @pl.loop(1, n)
    def _(step):
        y_copy(lax.rem(me + step, n), me).start()

    y_in[me] = y_out[me]

    @pl.loop(1, n)
    def _(step):
        y_copy(me, lax.rem(me + step, n)).wait_recv()

    branch = jnp.zeros((own_units, width), f32)
    for k in range(n):
        branch += y_in[k].astype(f32)
    mean_square = jnp.mean(branch * branch, axis=1, keepdims=True)
    normed = branch * lax.rsqrt(mean_square + 1e-06) * gain_ref[...]
    out_ref[...] = res_ref[...].astype(f32) + normed

    @pl.loop(1, half)
    def _(step):
        q_copy(me, sibling, step).wait_send()
        q_copy(me, sibling, half + step).wait_send()

    q_copy(me, sibling, 0).wait_send()

    @pl.loop(1, n)
    def _(step):
        target = lax.rem(me + step, n)
        for copy in part_copy(lax.div(target, owners), lax.rem(target, owners), me):
            copy.wait_send()
        y_copy(target, me).wait_send()


def shards(n, queries, keys, values, residual, post_gain, out_weight):
    kv_heads, context, head_dim = keys.shape
    own_units, all_width = queries.shape
    head_count = all_width // head_dim
    group_size = head_count // kv_heads
    own_rows = own_units * group_size
    rows = n * own_rows
    width = residual.shape[1]
    vmem = pl.BlockSpec(memory_space=pltpu.VMEM)
    hbm = pl.BlockSpec(memory_space=pl.ANY)
    dma = pltpu.SemaphoreType.DMA
    return pl.pallas_call(
        functools.partial(kernel, n, group_size),
        out_shape=jax.ShapeDtypeStruct((own_units, width), f32),
        in_specs=[vmem, hbm, hbm, vmem, vmem, hbm],
        out_specs=vmem,
        scratch_shapes=[
            pltpu.VMEM(keys.shape, bf16),
            pltpu.VMEM(values.shape, bf16),
            pltpu.VMEM(out_weight.shape, bf16),
            pltpu.VMEM((n, kv_heads, own_rows, head_dim), bf16),
            pltpu.VMEM((kv_heads, head_dim, rows), bf16),
            pltpu.VMEM((kv_heads, 8, rows), f32),
            pltpu.VMEM((n, head_dim, rows), bf16),
            pltpu.VMEM((n, 8, rows), f32),
            pltpu.VMEM((n, own_units, width), bf16),
            pltpu.VMEM((n, own_units, width), bf16),
            dma((kv_heads,)),
            dma((kv_heads,)),
            dma,
            dma((n,)),
            dma((n,)),
            dma((n,)),
            dma((n,)),
            dma((n,)),
            dma((n,)),
            dma((n,)),
            dma((n,)),
        ],
        compiler_params=pltpu.CompilerParams(
            collective_id=0, has_side_effects=True, vmem_limit_bytes=56 * 2**20
        ),
        cost_estimate=pl.CostEstimate(
            flops=4 * kv_heads * context * rows * head_dim,
            bytes_accessed=4 * kv_heads * context * head_dim,
            transcendentals=kv_heads * context * rows,
        ),
    )(queries, keys, values, residual, post_gain.reshape(1, width), out_weight)


def solution(mesh):
    in_specs = (
        P(("groups", "ctx"), None),
        P(None, ("groups", "ctx"), None),
        P(None, ("groups", "ctx"), None),
        P(("groups", "ctx"), None),
        P(),
        P("ctx", None),
    )
    out_specs = P(("groups", "ctx"), None)
    return jax.shard_map(
        functools.partial(shards, mesh.shape["ctx"]),
        mesh=mesh,
        in_specs=in_specs,
        out_specs=out_specs,
        check_vma=False,
    )
```

time: 327 us -> 53 us (0.16)
  the two profiles are of different devices: /device:TPU:0 before, /device:TPU:31 now
where the time goes in v1:
time: 53 us; the launch traced here: 52.7 us
  Pallas kernels  49.8 us (94%)
  local copies, waits for them, and re-layouts  2.89 us (5%)
    pallas_call x1, Pallas kernels, shards(): pl.pallas_call(functools.partial(kernel, n, group_size), out_shape=jax.Sh...  49.8 us
    unnamed x1, local copies, waits for them, and re-layouts  1.53 us
    reshape x1, local copies, waits for them, and re-layouts, shards(): post_gain.reshape(1, width)  1.36 us

profile of v1, /device:TPU:31, one launch (start us, length us, event | category | flops | bytes accessed | tf_op | source)
XLA Modules:
  0.0 52.7 jit_solution(446834358334051488)
XLA Ops:
  0.0 1.4 %reshape.3.gain_ref = f32[1,5376]{1,0:T(1,128)} reshape(f32[5376]{0:T(1024)} %param.10) | data formatting | bytes 43008 | tf_op jit(solution)/shard_map/reshape | solution.py:323
  1.4 49.8 %shard_map.64 = f32[4,5376]{1,0:T(4,128)} custom-call(bf16[4,4096]{1,0:T(4,128)(2,1)} %q_ref.1, bf16[16,2048,128]{2,1,0:T(8,128)(2,1)} %k_hbm.1, bf16[16,2048,128]{2,1,0:T(8,128)(2,1)} %v_hbm.1, bf16[4,5376]{1,0:T(4,128)(2,1)} %res_ref.1, f32[1,5376]{1,0:T(1,128)} %reshape.3.gain_ref, bf16[256,5376]{1,0:T(8,128)(2,1)} %w_hbm.1), custom_call_target="tpu_custom_call" | custom-call | flops 2147483648 | bytes 16777216 | tf_op jit(solution)/shard_map/pallas_call | solution.py:287
  51.2 1.5 %copy.8 = f32[4,5376]{1,0:T(4,128)} copy(f32[4,5376]{1,0:T(4,128)} %shard_map.64) | data formatting | bytes 172032

commit v2 on v1

--- a/solution.py
+++ b/solution.py
@@ -35,7 +35,11 @@
     part_in,
     stat_in,
     y_out,
-    y_in,
+    core_in,
+    across_out,
+    across_in,
+    z_out,
+    z_in,
     k_sem,
     v_sem,
     w_sem,
@@ -47,10 +51,20 @@
     s_recv,
     y_send,
     y_recv,
+    z_send,
+    z_recv,
 ):
     me = lax.axis_index("ctx")
     core = lax.rem(me, 2)
     sibling = me + 1 - 2 * core
+    depth = n // 4
+    y = lax.rem(lax.div(me, 2), 2)
+    z = lax.div(me, 4)
+
+    def device(its_z, its_y, its_core):
+        return (its_z * 2 + its_y) * 2 + its_core
+
+    across = device(z, 1 - y, core)
     kv_heads, context, head_dim = k_buf.shape
     own_units = q_ref.shape[0]
     owners = n // kv_heads
@@ -107,26 +121,32 @@
             device_id_type=MESH,
         )
 
-    half = n // 2
-
-    def peer(step):
-        return lax.rem(me + 2 * step, n)
-
-    @pl.loop(1, half)
-    def _(step):
-        q_copy(me, peer(step), step).start()
-
-    q_copy(me, sibling, 0).start()
-
-    @pl.loop(1, half)
-    def _(step):
-        source = peer(half - step)
+    def at_z(step, its_y):
+        return device(lax.rem(z + step, depth), its_y, core)
+
+    @pl.loop(1, depth)
+    def _(step):
+        q_copy(me, at_z(step, y), step).start()
+
+    q_copy(me, across, 0).start()
+    q_copy(me, sibling, depth).start()
+
+    @pl.loop(1, depth)
+    def _(step):
+        source = at_z(depth - step, y)
         q_copy(source, sibling, 0).wait_recv()
-        q_copy(source, sibling, half + step).start()
-
-    @pl.loop(0, half)
-    def _(step):
-        q_copy(lax.rem(sibling + 2 * step, n), sibling, 0).wait_recv()
+        q_copy(source, across, 2 * depth + step).start()
+        q_copy(source, sibling, depth + step).start()
+
+    @pl.loop(0, depth)
+    def _(step):
+        source = at_z(depth - step, 1 - y)
+        q_copy(source, sibling, 0).wait_recv()
+        q_copy(source, sibling, 3 * depth + step).start()
+
+    @pl.loop(0, n // 2)
+    def _(step):
+        q_copy(2 * step + 1 - core, sibling, 0).wait_recv()
 
     def part_copy(h, p, source):
         slot = h * owners + p
@@ -225,52 +245,98 @@
     own_block = jnp.concatenate(blocks, axis=1) if own_heads > 1 else blocks[0]
 
     w_copy.wait()
-    step_width = chunk_of(width, 1024)
-    for c in range(0, width, step_width):
-        y = jnp.dot(own_block, w_buf[:, c : c + step_width], preferred_element_type=f32)
+
+    def core_copy(c):
+        return pltpu.make_async_remote_copy(
+            src_ref=y_out.at[c, 1 - core],
+            dst_ref=core_in.at[c],
+            send_sem=y_send.at[0, c],
+            recv_sem=y_recv.at[0, c],
+            device_id={"ctx": sibling},
+            device_id_type=MESH,
+        )
+
+    def across_copy(c):
+        return pltpu.make_async_remote_copy(
+            src_ref=across_out.at[c],
+            dst_ref=across_in.at[c],
+            send_sem=y_send.at[1, c],
+            recv_sem=y_recv.at[1, c],
+            device_id={"ctx": across},
+            device_id_type=MESH,
+        )
+
+    def z_copy(c, target, source):
+        return pltpu.make_async_remote_copy(
+            src_ref=z_out.at[c, target],
+            dst_ref=z_in.at[c, source],
+            send_sem=z_send.at[c, target],
+            recv_sem=z_recv.at[c, source],
+            device_id={"ctx": device(target, y, core)},
+            device_id_type=MESH,
+        )
+
+    chunks = y_out.shape[0]
+    cols = y_out.shape[-1]
+    for c in range(chunks):
+        product = jnp.dot(
+            own_block, w_buf[:, c * cols : (c + 1) * cols], preferred_element_type=f32
+        )
         for k in range(n):
-            y_out[k, :, c : c + step_width] = y[k * own_units : (k + 1) * own_units].astype(bf16)
-
-    def y_copy(target, source):
-        return pltpu.make_async_remote_copy(
-            src_ref=y_out.at[target],
-            dst_ref=y_in.at[source],
-            send_sem=y_send.at[target],
-            recv_sem=y_recv.at[source],
-            device_id={"ctx": target},
-            device_id_type=MESH,
-        )
-
-    @pl.loop(1, n)
-    def _(step):
-        y_copy(lax.rem(me + step, n), me).start()
-
-    y_in[me] = y_out[me]
-
-    @pl.loop(1, n)
-    def _(step):
-        y_copy(me, lax.rem(me + step, n)).wait_recv()
-
-    branch = jnp.zeros((own_units, width), f32)
-    for k in range(n):
-        branch += y_in[k].astype(f32)
-    mean_square = jnp.mean(branch * branch, axis=1, keepdims=True)
-    normed = branch * lax.rsqrt(mean_square + 1e-06) * gain_ref[...]
-    out_ref[...] = res_ref[...].astype(f32) + normed
-
-    @pl.loop(1, half)
-    def _(step):
-        q_copy(me, sibling, step).wait_send()
-        q_copy(me, sibling, half + step).wait_send()
-
-    q_copy(me, sibling, 0).wait_send()
+            y_out[c, k % 2, k // 2 % 2, k // 4] = product[
+                k * own_units : (k + 1) * own_units
+            ].astype(bf16)
+        core_copy(c).start()
+    for c in range(chunks):
+        core_copy(c).wait_recv()
+        across_out[c] = (
+            y_out[c, core, 1 - y].astype(f32) + core_in[c, 1 - y].astype(f32)
+        ).astype(bf16)
+        across_copy(c).start()
+    for c in range(chunks):
+        own_sum = y_out[c, core, y].astype(f32) + core_in[c, y].astype(f32)
+        across_copy(c).wait_recv()
+        z_out[c] = (own_sum + across_in[c].astype(f32)).astype(bf16)
+
+        @pl.loop(1, depth)
+        def _(step):
+            z_copy(c, lax.rem(z + step, depth), z).start()
+
+        z_in[c, z] = z_out[c, z]
+    branches = []
+    for c in range(chunks):
+
+        @pl.loop(1, depth)
+        def _(step):
+            z_copy(c, z, lax.rem(z + step, depth)).wait_recv()
+
+        branches.append(jnp.sum(z_in[c].astype(f32), axis=0))
+    squares = sum(jnp.sum(b * b, axis=1, keepdims=True) for b in branches)
+    inverse = lax.rsqrt(squares / width + 1e-06)
+    for c, branch in enumerate(branches):
+        at = pl.ds(c * cols, cols)
+        gain = gain_ref[at].reshape(1, cols)
+        out_ref[:, at] = res_ref[:, at].astype(f32) + branch * inverse * gain
+
+    @pl.loop(0, n)
+    def _(step):
+        @pl.when(step != 2 * depth)
+        def _():
+            q_copy(me, sibling, step).wait_send()
 
     @pl.loop(1, n)
     def _(step):
         target = lax.rem(me + step, n)
         for copy in part_copy(lax.div(target, owners), lax.rem(target, owners), me):
             copy.wait_send()
-        y_copy(target, me).wait_send()
+
+    for c in range(chunks):
+        core_copy(c).wait_send()
+        across_copy(c).wait_send()
+
+        @pl.loop(1, depth)
+        def _(step):
+            z_copy(c, lax.rem(z + step, depth), z).wait_send()
 
 
 def shards(n, queries, keys, values, residual, post_gain, out_weight):
@@ -281,6 +347,9 @@
     own_rows = own_units * group_size
     rows = n * own_rows
     width = residual.shape[1]
+    cols = chunk_of(width, 2048)
+    chunks = width // cols
+    depth = n // 4
     vmem = pl.BlockSpec(memory_space=pltpu.VMEM)
     hbm = pl.BlockSpec(memory_space=pl.ANY)
     dma = pltpu.SemaphoreType.DMA
@@ -298,8 +367,12 @@
             pltpu.VMEM((kv_heads, 8, rows), f32),
             pltpu.VMEM((n, head_dim, rows), bf16),
             pltpu.VMEM((n, 8, rows), f32),
-            pltpu.VMEM((n, own_units, width), bf16),
-            pltpu.VMEM((n, own_units, width), bf16),
+            pltpu.VMEM((chunks, 2, 2, depth, own_units, cols), bf16),
+            pltpu.VMEM((chunks, 2, depth, own_units, cols), bf16),
+            pltpu.VMEM((chunks, depth, own_units, cols), bf16),
+            pltpu.VMEM((chunks, depth, own_units, cols), bf16),
+            pltpu.VMEM((chunks, depth, own_units, cols), bf16),
+            pltpu.VMEM((chunks, depth, own_units, cols), bf16),
             dma((kv_heads,)),
             dma((kv_heads,)),
             dma,
@@ -309,8 +382,10 @@
             dma((n,)),
             dma((n,)),
             dma((n,)),
-            dma((n,)),
-            dma((n,)),
+            dma((2, chunks)),
+            dma((2, chunks)),
+            dma((chunks, depth)),
+            dma((chunks, depth)),
         ],
         compiler_params=pltpu.CompilerParams(
             collective_id=0, has_side_effects=True, vmem_limit_bytes=56 * 2**20
@@ -320,7 +395,7 @@
             bytes_accessed=4 * kv_heads * context * head_dim,
             transcendentals=kv_heads * context * rows,
         ),
-    )(queries, keys, values, residual, post_gain.reshape(1, width), out_weight)
+    )(queries, keys, values, residual, post_gain, out_weight)
 
 
 def solution(mesh):

time: 53 us -> 47.2 us (0.89)
  the two profiles are of different devices: /device:TPU:31 before, /device:TPU:0 now
where the time goes in v2:
time: 47.2 us; the launch traced here: 47 us
  Pallas kernels  45.5 us (96%)
  local copies, waits for them, and re-layouts  1.53 us (3%)
    pallas_call x1, Pallas kernels, shards(): pl.pallas_call(functools.partial(kernel, n, group_size), out_shape=jax.Sh...  45.5 us
    unnamed x1, local copies, waits for them, and re-layouts  1.53 us

profile of v2, /device:TPU:0, one launch (start us, length us, event | category | flops | bytes accessed | tf_op | source)
XLA Modules:
  0.0 47.0 jit_solution(13763769311300556310)
XLA Ops:
  0.0 45.5 %shard_map.64 = f32[4,5376]{1,0:T(4,128)} custom-call(bf16[4,4096]{1,0:T(4,128)(2,1)} %q_ref.1, bf16[16,2048,128]{2,1,0:T(8,128)(2,1)} %k_hbm.1, bf16[16,2048,128]{2,1,0:T(8,128)(2,1)} %v_hbm.1, bf16[4,5376]{1,0:T(4,128)(2,1)} %res_ref.1, f32[5376]{0:T(1024)} %gain_ref.1, bf16[256,5376]{1,0:T(8,128)(2,1)} %w_hbm.1), custom_call_target="tpu_custom_call" | custom-call | flops 2147483648 | bytes 16777216 | tf_op jit(solution)/shard_map/pallas_call | solution.py:356
  45.5 1.5 %copy.8 = f32[4,5376]{1,0:T(4,128)} copy(f32[4,5376]{1,0:T(4,128)} %shard_map.64) | data formatting | bytes 172032

commit v3 on v2

--- a/solution.py
+++ b/solution.py
@@ -171,44 +171,62 @@
 
     tile = chunk_of(context, 512)
 
-    @pl.loop(0, kv_heads)
-    def _(step):
-        h = head_at(step)
-        q = q_all[:, h].astype(f32).reshape(rows, head_dim).astype(bf16)
-        k_copy(h).wait()
-        scores = [
-            lax.dot_general(
-                k_buf[h, pl.ds(t, tile), :],
+    def queries_of(h):
+        return q_all[:, h].astype(f32).reshape(rows, head_dim).astype(bf16)
+
+    def merged(peaks, totals, parts):
+        peak = functools.reduce(jnp.maximum, peaks)
+        factors = [jnp.exp2(p - peak) for p in peaks]
+        total = sum(f * t for f, t in zip(factors, totals))
+        return peak, total, sum(f * w for f, w in zip(factors, parts))
+
+    @pl.loop(0, kv_heads // 2)
+    def _(step):
+        heads = [head_at(2 * step), head_at(2 * step + 1)]
+        empty = jnp.zeros((rows, head_dim), bf16)
+        q0, q1 = [queries_of(h) for h in heads]
+        q = jnp.concatenate(
+            [jnp.concatenate([q0, empty], axis=1), jnp.concatenate([empty, q1], axis=1)], axis=0
+        )
+        for h in heads:
+            k_copy(h).wait()
+            v_copy(h).wait()
+        peaks, totals, parts = ([], []), ([], []), ([], [])
+        for t in range(0, context, tile):
+            at = pl.ds(t, tile)
+            scores = lax.dot_general(
+                jnp.concatenate([k_buf[h, at, :] for h in heads], axis=1),
                 q,
                 (((1,), (1,)), ((), ())),
                 preferred_element_type=f32,
             )
-            for t in range(0, context, tile)
-        ]
-        peak = functools.reduce(
-            jnp.maximum, [jnp.max(s, axis=0, keepdims=True) for s in scores]
-        ) * scale
-        v_copy(h).wait()
-        total = jnp.zeros((1, rows), f32)
-        weighted = jnp.zeros((head_dim, rows), f32)
-        for i, s in enumerate(scores):
-            exponent = jnp.exp2(s * scale - peak)
-            total += jnp.sum(exponent, axis=0, keepdims=True)
-            weighted += lax.dot_general(
-                v_buf[h, pl.ds(i * tile, tile), :],
-                exponent.astype(bf16),
-                (((0,), (0,)), ((), ())),
-                preferred_element_type=f32,
-            )
+            peak = jnp.max(scores, axis=0, keepdims=True) * scale
+            exponent = jnp.exp2(scores * scale - peak)
+            total = jnp.sum(exponent, axis=0, keepdims=True)
+            weights = exponent.astype(bf16)
+            for i, h in enumerate(heads):
+                mine = slice(i * rows, (i + 1) * rows)
+                peaks[i].append(peak[:, mine])
+                totals[i].append(total[:, mine])
+                parts[i].append(
+                    lax.dot_general(
+                        v_buf[h, at, :],
+                        weights[:, mine],
+                        (((0,), (0,)), ((), ())),
+                        preferred_element_type=f32,
+                    )
+                )
         row = lax.broadcasted_iota(jnp.int32, (8, rows), 0)
-        part_out[h] = weighted.astype(bf16)
-        stat_out[h] = jnp.where(row == 0, peak, total)
-        for p in range(owners):
-
-            @pl.when(h * owners + p != me)
-            def _():
-                for copy in part_copy(h, p, me):
-                    copy.start()
+        for i, h in enumerate(heads):
+            peak, total, weighted = merged(peaks[i], totals[i], parts[i])
+            part_out[h] = weighted.astype(bf16)
+            stat_out[h] = jnp.where(row == 0, peak, total)
+            for p in range(owners):
+
+                @pl.when(h * owners + p != me)
+                def _():
+                    for copy in part_copy(h, p, me):
+                        copy.start()
 
     part_in[me] = part_out[own_head]
     stat_in[me] = stat_out[own_head]

time: 47.2 us -> 47.9 us (1.015)
  Pallas kernels: 45.5 us -> 46.2 us
    pallas_call x1, Pallas kernels: 45.5 us -> 46.2 us  [shards(): pl.pallas_call(functools.partial(kernel, n, group_size), out_shape=jax.Sh...]
where the time goes in v3:
time: 47.9 us; the launch traced here: 47.7 us
  Pallas kernels  46.2 us (96%)
  local copies, waits for them, and re-layouts  1.53 us (3%)
    pallas_call x1, Pallas kernels, shards(): pl.pallas_call(functools.partial(kernel, n, group_size), out_shape=jax.Sh...  46.2 us
    unnamed x1, local copies, waits for them, and re-layouts  1.53 us

profile of v3, /device:TPU:0, one launch (start us, length us, event | category | flops | bytes accessed | tf_op | source)
XLA Modules:
  0.0 47.7 jit_solution(17080695465391616842)
XLA Ops:
  0.0 46.2 %shard_map.64 = f32[4,5376]{1,0:T(4,128)} custom-call(bf16[4,4096]{1,0:T(4,128)(2,1)} %q_ref.1, bf16[16,2048,128]{2,1,0:T(8,128)(2,1)} %k_hbm.1, bf16[16,2048,128]{2,1,0:T(8,128)(2,1)} %v_hbm.1, bf16[4,5376]{1,0:T(4,128)(2,1)} %res_ref.1, f32[5376]{0:T(1024)} %gain_ref.1, bf16[256,5376]{1,0:T(8,128)(2,1)} %w_hbm.1), custom_call_target="tpu_custom_call" | custom-call | flops 2147483648 | bytes 16777216 | tf_op jit(solution)/shard_map/pallas_call | solution.py:374
  46.2 1.5 %copy.8 = f32[4,5376]{1,0:T(4,128)} copy(f32[4,5376]{1,0:T(4,128)} %shard_map.64) | data formatting | bytes 172032

commit v4 on v3

--- a/solution.py
+++ b/solution.py
@@ -169,58 +169,43 @@
             ),
         )
 
-    tile = chunk_of(context, 512)
+    tile = chunk_of(context, 1024)
 
     def queries_of(h):
         return q_all[:, h].astype(f32).reshape(rows, head_dim).astype(bf16)
 
-    def merged(peaks, totals, parts):
+    def attend(h):
+        q = queries_of(h)
+        peaks, totals, parts = [], [], []
+        for t in range(0, context, tile):
+            at = pl.ds(t, tile)
+            scores = lax.dot_general(
+                q, k_buf[h, at, :], (((1,), (1,)), ((), ())), preferred_element_type=f32
+            )
+            peak = jnp.max(scores, axis=1, keepdims=True) * scale
+            exponent = jnp.exp2(scores * scale - peak)
+            peaks.append(peak)
+            totals.append(jnp.sum(exponent, axis=1, keepdims=True))
+            parts.append(
+                jnp.dot(exponent.astype(bf16), v_buf[h, at, :], preferred_element_type=f32)
+            )
         peak = functools.reduce(jnp.maximum, peaks)
         factors = [jnp.exp2(p - peak) for p in peaks]
         total = sum(f * t for f, t in zip(factors, totals))
-        return peak, total, sum(f * w for f, w in zip(factors, parts))
+        weighted = sum(f * w for f, w in zip(factors, parts))
+        lane = lax.broadcasted_iota(jnp.int32, (rows, 128), 1)
+        part_out[h] = weighted.astype(bf16)
+        stat_out[h] = jnp.where(lane == 0, peak, total).T[0:8]
 
     @pl.loop(0, kv_heads // 2)
     def _(step):
         heads = [head_at(2 * step), head_at(2 * step + 1)]
-        empty = jnp.zeros((rows, head_dim), bf16)
-        q0, q1 = [queries_of(h) for h in heads]
-        q = jnp.concatenate(
-            [jnp.concatenate([q0, empty], axis=1), jnp.concatenate([empty, q1], axis=1)], axis=0
-        )
         for h in heads:
             k_copy(h).wait()
             v_copy(h).wait()
-        peaks, totals, parts = ([], []), ([], []), ([], [])
-        for t in range(0, context, tile):
-            at = pl.ds(t, tile)
-            scores = lax.dot_general(
-                jnp.concatenate([k_buf[h, at, :] for h in heads], axis=1),
-                q,
-                (((1,), (1,)), ((), ())),
-                preferred_element_type=f32,
-            )
-            peak = jnp.max(scores, axis=0, keepdims=True) * scale
-            exponent = jnp.exp2(scores * scale - peak)
-            total = jnp.sum(exponent, axis=0, keepdims=True)
-            weights = exponent.astype(bf16)
-            for i, h in enumerate(heads):
-                mine = slice(i * rows, (i + 1) * rows)
-                peaks[i].append(peak[:, mine])
-                totals[i].append(total[:, mine])
-                parts[i].append(
-                    lax.dot_general(
-                        v_buf[h, at, :],
-                        weights[:, mine],
-                        (((0,), (0,)), ((), ())),
-                        preferred_element_type=f32,
-                    )
-                )
-        row = lax.broadcasted_iota(jnp.int32, (8, rows), 0)
-        for i, h in enumerate(heads):
-            peak, total, weighted = merged(peaks[i], totals[i], parts[i])
-            part_out[h] = weighted.astype(bf16)
-            stat_out[h] = jnp.where(row == 0, peak, total)
+        for h in heads:
+            attend(h)
+        for h in heads:
             for p in range(owners):
 
                 @pl.when(h * owners + p != me)
@@ -236,15 +221,10 @@
         for copy in part_copy(0, 0, lax.rem(me + step, n)):
             copy.wait_recv()
 
-    stats = stat_in[...]
-    overall = jnp.max(stats, axis=0)[0:1, :]
-    total = jnp.zeros((1, rows), f32)
-    weighted = jnp.zeros((head_dim, rows), f32)
-    for k in range(n):
-        factor = jnp.exp2(stats[k, 0:1, :] - overall)
-        total += factor * stats[k, 1:2, :]
-        weighted += factor * part_in[k].astype(f32)
-    attended = (weighted / total).astype(bf16)
+    peaks, totals = stat_in[:, 0, :], stat_in[:, 1, :]
+    factors = jnp.exp2(peaks - jnp.max(peaks, axis=0, keepdims=True))
+    shares = (factors / jnp.sum(factors * totals, axis=0, keepdims=True)).T
+    attended = sum(shares[:, k : k + 1] * part_in[k].astype(f32) for k in range(n)).astype(bf16)
 
     unit = lax.broadcasted_iota(jnp.int32, (units, rows), 0)
     column = lax.broadcasted_iota(jnp.int32, (units, rows), 1)
@@ -256,9 +236,7 @@
         )
         pick = jnp.where(column == place, 1.0, 0.0).astype(bf16)
         blocks.append(
-            lax.dot_general(
-                pick, attended, (((1,), (1,)), ((), ())), preferred_element_type=f32
-            ).astype(bf16)
+            jnp.dot(pick, attended, preferred_element_type=f32).astype(bf16)
         )
     own_block = jnp.concatenate(blocks, axis=1) if own_heads > 1 else blocks[0]
 
@@ -381,9 +359,9 @@
             pltpu.VMEM(values.shape, bf16),
             pltpu.VMEM(out_weight.shape, bf16),
             pltpu.VMEM((n, kv_heads, own_rows, head_dim), bf16),
-            pltpu.VMEM((kv_heads, head_dim, rows), bf16),
+            pltpu.VMEM((kv_heads, rows, head_dim), bf16),
             pltpu.VMEM((kv_heads, 8, rows), f32),
-            pltpu.VMEM((n, head_dim, rows), bf16),
+            pltpu.VMEM((n, rows, head_dim), bf16),
             pltpu.VMEM((n, 8, rows), f32),
             pltpu.VMEM((chunks, 2, 2, depth, own_units, cols), bf16),
             pltpu.VMEM((chunks, 2, depth, own_units, cols), bf16),

time: 47.9 us -> 48.7 us (1.017)
  Pallas kernels: 46.2 us -> 47 us
    pallas_call x1, Pallas kernels: 46.2 us -> 47 us  [shards(): pl.pallas_call(functools.partial(kernel, n, group_size), out_shape=jax.Sh...]
where the time goes in v4:
time: 48.7 us; the launch traced here: 48.5 us
  Pallas kernels  47 us (97%)
  local copies, waits for them, and re-layouts  1.53 us (3%)
    pallas_call x1, Pallas kernels, shards(): pl.pallas_call(functools.partial(kernel, n, group_size), out_shape=jax.Sh...  47 us
    unnamed x1, local copies, waits for them, and re-layouts  1.53 us

profile of v4, /device:TPU:0, one launch (start us, length us, event | category | flops | bytes accessed | tf_op | source)
XLA Modules:
  0.0 48.5 jit_solution(2872322896669650348)
XLA Ops:
  0.0 47.0 %shard_map.64 = f32[4,5376]{1,0:T(4,128)} custom-call(bf16[4,4096]{1,0:T(4,128)(2,1)} %q_ref.1, bf16[16,2048,128]{2,1,0:T(8,128)(2,1)} %k_hbm.1, bf16[16,2048,128]{2,1,0:T(8,128)(2,1)} %v_hbm.1, bf16[4,5376]{1,0:T(4,128)(2,1)} %res_ref.1, f32[5376]{0:T(1024)} %gain_ref.1, bf16[256,5376]{1,0:T(8,128)(2,1)} %w_hbm.1), custom_call_target="tpu_custom_call" | custom-call | flops 2147483648 | bytes 16777216 | tf_op jit(solution)/shard_map/pallas_call | solution.py:352
  47.0 1.5 %copy.8 = f32[4,5376]{1,0:T(4,128)} copy(f32[4,5376]{1,0:T(4,128)} %shard_map.64) | data formatting | bytes 172032

commit v5 on v2

--- a/solution.py
+++ b/solution.py
@@ -30,10 +30,14 @@
     v_buf,
     w_buf,
     q_all,
-    part_out,
-    stat_out,
-    part_in,
-    stat_in,
+    core_out,
+    core_got,
+    cross_out,
+    cross_got,
+    deep_out,
+    deep_got,
+    mine_weighted,
+    mine_stat,
     y_out,
     core_in,
     across_out,
@@ -47,8 +51,6 @@
     q_recv,
     p_send,
     p_recv,
-    s_send,
-    s_recv,
     y_send,
     y_recv,
     z_send,
@@ -74,10 +76,19 @@
     units = n * own_units
     width = w_buf.shape[1]
     scale = 168.0**-0.5 * math.log2(math.e)
-    own_head = lax.div(me, owners)
+    chips = n // 2
+
+    def place_at(rank):
+        its_y = jnp.where(rank < depth, 1 - y, y)
+        return lax.rem(z + 1 + rank, depth), its_y
 
     def head_at(step):
-        return lax.rem(own_head + 1 + step, kv_heads)
+        rank = lax.rem(step, chips)
+        its_z, its_y = place_at(rank)
+        chip = its_z * 2 + its_y
+        if owners > 1:
+            return chip
+        return chip * 2 + jnp.where(step < chips, 1 - core, core)
 
     def k_copy(h):
         return pltpu.make_async_copy(k_hbm.at[h], k_buf.at[h], k_sem.at[h])
@@ -96,11 +107,15 @@
 
     barrier = pltpu.get_barrier_semaphore()
 
-    @pl.loop(1, n)
-    def _(step):
-        pl.semaphore_signal(
-            barrier, inc=1, device_id={"ctx": lax.rem(me + step, n)}, device_id_type=MESH
-        )
+    def greet(target):
+        pl.semaphore_signal(barrier, inc=1, device_id={"ctx": target}, device_id_type=MESH)
+
+    greet(sibling)
+    greet(across)
+
+    @pl.loop(1, depth)
+    def _(step):
+        greet(device(lax.rem(z + step, depth), y, core))
 
     own = q_ref[...].astype(f32)
     for h in range(kv_heads):
@@ -109,7 +124,7 @@
             [own[:, first + g * head_dim :][:, :head_dim] for g in range(group_size)], axis=0
         ).astype(bf16)
 
-    pl.semaphore_wait(barrier, n - 1)
+    pl.semaphore_wait(barrier, depth + 1)
 
     def q_copy(block, target, slot):
         return pltpu.make_async_remote_copy(
@@ -148,84 +163,124 @@
     def _(step):
         q_copy(2 * step + 1 - core, sibling, 0).wait_recv()
 
-    def part_copy(h, p, source):
-        slot = h * owners + p
-        return (
+    def part_copies(target, out, into, kind, slot, landing):
+        return [
             pltpu.make_async_remote_copy(
-                src_ref=part_out.at[h],
-                dst_ref=part_in.at[source],
-                send_sem=p_send.at[slot],
-                recv_sem=p_recv.at[source],
-                device_id={"ctx": slot},
+                src_ref=source,
+                dst_ref=destination,
+                send_sem=p_send.at[kind, i, slot],
+                recv_sem=p_recv.at[kind, i, landing],
+                device_id={"ctx": target},
                 device_id_type=MESH,
-            ),
-            pltpu.make_async_remote_copy(
-                src_ref=stat_out.at[h],
-                dst_ref=stat_in.at[source],
-                send_sem=s_send.at[slot],
-                recv_sem=s_recv.at[source],
-                device_id={"ctx": slot},
-                device_id_type=MESH,
-            ),
-        )
+            )
+            for i, (source, destination) in enumerate(zip(out, into))
+        ]
+
+    def at(refs, i):
+        return [ref.at[i] for ref in refs]
+
+    def to_core(chip):
+        return part_copies(sibling, at(core_out, chip), at(core_got, chip), 0, chip, chip)
+
+    def to_across(its_z):
+        return part_copies(across, at(cross_out, its_z), at(cross_got, its_z), 1, its_z, its_z)
+
+    def to_z(target, source):
+        return part_copies(
+            device(target, y, core), at(deep_out, target), at(deep_got, source), 2, target, source
+        )
+
+    def start(copies):
+        for copy in copies:
+            copy.start()
+
+    def put(refs, i, partial):
+        peak, total, weighted = partial
+        row = lax.broadcasted_iota(jnp.int32, (8, rows), 0)
+        refs[0][i] = weighted.astype(bf16)
+        refs[1][i] = jnp.where(row == 0, peak, total)
+
+    def get(refs, i):
+        return refs[1][i, 0:1, :], refs[1][i, 1:2, :], refs[0][i].astype(f32)
+
+    def merge(partials):
+        peak = functools.reduce(jnp.maximum, [p for p, _, _ in partials])
+        factors = [jnp.exp2(p - peak) for p, _, _ in partials]
+        total = sum(f * t for f, (_, t, _) in zip(factors, partials))
+        return peak, total, sum(f * w for f, (_, _, w) in zip(factors, partials))
 
     tile = chunk_of(context, 512)
 
     @pl.loop(0, kv_heads)
     def _(step):
         h = head_at(step)
+        rank = lax.rem(step, chips)
+        its_z, its_y = place_at(rank)
+        chip = its_z * 2 + its_y
         q = q_all[:, h].astype(f32).reshape(rows, head_dim).astype(bf16)
         k_copy(h).wait()
-        scores = [
-            lax.dot_general(
+        v_copy(h).wait()
+        partials = []
+        for t in range(0, context, tile):
+            scores = lax.dot_general(
                 k_buf[h, pl.ds(t, tile), :],
                 q,
                 (((1,), (1,)), ((), ())),
                 preferred_element_type=f32,
             )
-            for t in range(0, context, tile)
-        ]
-        peak = functools.reduce(
-            jnp.maximum, [jnp.max(s, axis=0, keepdims=True) for s in scores]
-        ) * scale
-        v_copy(h).wait()
-        total = jnp.zeros((1, rows), f32)
-        weighted = jnp.zeros((head_dim, rows), f32)
-        for i, s in enumerate(scores):
-            exponent = jnp.exp2(s * scale - peak)
-            total += jnp.sum(exponent, axis=0, keepdims=True)
-            weighted += lax.dot_general(
-                v_buf[h, pl.ds(i * tile, tile), :],
+            peak = jnp.max(scores, axis=0, keepdims=True) * scale
+            exponent = jnp.exp2(scores * scale - peak)
+            total = jnp.sum(exponent, axis=0, keepdims=True)
+            weighted = lax.dot_general(
+                v_buf[h, pl.ds(t, tile), :],
                 exponent.astype(bf16),
                 (((0,), (0,)), ((), ())),
                 preferred_element_type=f32,
             )
-        row = lax.broadcasted_iota(jnp.int32, (8, rows), 0)
-        part_out[h] = weighted.astype(bf16)
-        stat_out[h] = jnp.where(row == 0, peak, total)
-        for p in range(owners):
-
-            @pl.when(h * owners + p != me)
+            partials.append((peak, total, weighted))
+        peak, total, weighted = merge(partials)
+        mine_weighted[...] = weighted
+        mine_stat[0:1, :] = peak
+        mine_stat[1:2, :] = total
+
+        def mine():
+            return mine_stat[0:1, :], mine_stat[1:2, :], mine_weighted[...]
+
+        @pl.when((step < chips) if owners == 1 else (step >= 0))
+        def _():
+            put(core_out, chip, mine())
+            start(to_core(chip))
+
+        @pl.when((step >= chips) if owners == 1 else (step >= 0))
+        def _():
+            for copy in to_core(chip):
+                copy.wait_recv()
+            two = merge([mine(), get(core_got, chip)])
+
+            @pl.when(rank < depth)
             def _():
-                for copy in part_copy(h, p, me):
-                    copy.start()
-
-    part_in[me] = part_out[own_head]
-    stat_in[me] = stat_out[own_head]
-
-    @pl.loop(1, n)
-    def _(step):
-        for copy in part_copy(0, 0, lax.rem(me + step, n)):
+                put(cross_out, its_z, two)
+                start(to_across(its_z))
+
+            @pl.when(rank >= depth)
+            def _():
+                for copy in to_across(its_z):
+                    copy.wait_recv()
+                put(deep_out, its_z, merge([two, get(cross_got, its_z)]))
+
+                @pl.when(its_z != z)
+                def _():
+                    start(to_z(its_z, z))
+
+    deep_got[0][z] = deep_out[0][z]
+    deep_got[1][z] = deep_out[1][z]
+
+    @pl.loop(1, depth)
+    def _(step):
+        for copy in to_z(z, lax.rem(z + step, depth)):
             copy.wait_recv()
 
-    stats = stat_in[...]
-    overall = jnp.max(stats, axis=0)[0:1, :]
-    total = jnp.zeros((1, rows), f32)
-    weighted = jnp.zeros((head_dim, rows), f32)
-    for k in range(n):
-        factor = jnp.exp2(stats[k, 0:1, :] - overall)
-        total += factor * stats[k, 1:2, :]
-        weighted += factor * part_in[k].astype(f32)
+    _, total, weighted = merge([get(deep_got, i) for i in range(depth)])
     attended = (weighted / total).astype(bf16)
 
     unit = lax.broadcasted_iota(jnp.int32, (units, rows), 0)
@@ -314,9 +369,9 @@
     squares = sum(jnp.sum(b * b, axis=1, keepdims=True) for b in branches)
     inverse = lax.rsqrt(squares / width + 1e-06)
     for c, branch in enumerate(branches):
-        at = pl.ds(c * cols, cols)
-        gain = gain_ref[at].reshape(1, cols)
-        out_ref[:, at] = res_ref[:, at].astype(f32) + branch * inverse * gain
+        span = pl.ds(c * cols, cols)
+        gain = gain_ref[span].reshape(1, cols)
+        out_ref[:, span] = res_ref[:, span].astype(f32) + branch * inverse * gain
 
     @pl.loop(0, n)
     def _(step):
@@ -324,11 +379,20 @@
         def _():
             q_copy(me, sibling, step).wait_send()
 
-    @pl.loop(1, n)
-    def _(step):
-        target = lax.rem(me + step, n)
-        for copy in part_copy(lax.div(target, owners), lax.rem(target, owners), me):
+    @pl.loop(0, chips)
+    def _(chip):
+        for copy in to_core(chip):
             copy.wait_send()
+
+    @pl.loop(0, depth)
+    def _(its_z):
+        for copy in to_across(its_z):
+            copy.wait_send()
+
+        @pl.when(its_z != z)
+        def _():
+            for copy in to_z(its_z, z):
+                copy.wait_send()
 
     for c in range(chunks):
         core_copy(c).wait_send()
@@ -353,6 +417,13 @@
     vmem = pl.BlockSpec(memory_space=pltpu.VMEM)
     hbm = pl.BlockSpec(memory_space=pl.ANY)
     dma = pltpu.SemaphoreType.DMA
+
+    def partials(count):
+        return [
+            pltpu.VMEM((count, head_dim, rows), bf16),
+            pltpu.VMEM((count, 8, rows), f32),
+        ]
+
     return pl.pallas_call(
         functools.partial(kernel, n, group_size),
         out_shape=jax.ShapeDtypeStruct((own_units, width), f32),
@@ -363,10 +434,14 @@
             pltpu.VMEM(values.shape, bf16),
             pltpu.VMEM(out_weight.shape, bf16),
             pltpu.VMEM((n, kv_heads, own_rows, head_dim), bf16),
-            pltpu.VMEM((kv_heads, head_dim, rows), bf16),
-            pltpu.VMEM((kv_heads, 8, rows), f32),
-            pltpu.VMEM((n, head_dim, rows), bf16),
-            pltpu.VMEM((n, 8, rows), f32),
+            partials(n // 2),
+            partials(n // 2),
+            partials(depth),
+            partials(depth),
+            partials(depth),
+            partials(depth),
+            pltpu.VMEM((head_dim, rows), f32),
+            pltpu.VMEM((8, rows), f32),
             pltpu.VMEM((chunks, 2, 2, depth, own_units, cols), bf16),
             pltpu.VMEM((chunks, 2, depth, own_units, cols), bf16),
             pltpu.VMEM((chunks, depth, own_units, cols), bf16),
@@ -378,10 +453,8 @@
             dma,
             dma((n,)),
             dma((n,)),
-            dma((n,)),
-            dma((n,)),
-            dma((n,)),
-            dma((n,)),
+            dma((3, 2, n // 2)),
+            dma((3, 2, n // 2)),
             dma((2, chunks)),
             dma((2, chunks)),
             dma((chunks, depth)),

time: 47.2 us -> 46.9 us (level)
  no operation moved by 1% of the time
where the time goes in v5:
time: 46.9 us; the launch traced here: 46.7 us
  Pallas kernels  45.1 us (96%)
  local copies, waits for them, and re-layouts  1.53 us (3%)
    pallas_call x1, Pallas kernels, shards(): pl.pallas_call(functools.partial(kernel, n, group_size), out_shape=jax.Sh...  45.1 us
    unnamed x1, local copies, waits for them, and re-layouts  1.53 us

profile of v5, /device:TPU:0, one launch (start us, length us, event | category | flops | bytes accessed | tf_op | source)
XLA Modules:
  0.0 46.7 jit_solution(10365868141157722166)
XLA Ops:
  0.0 45.1 %shard_map.64 = f32[4,5376]{1,0:T(4,128)} custom-call(bf16[4,4096]{1,0:T(4,128)(2,1)} %q_ref.1, bf16[16,2048,128]{2,1,0:T(8,128)(2,1)} %k_hbm.1, bf16[16,2048,128]{2,1,0:T(8,128)(2,1)} %v_hbm.1, bf16[4,5376]{1,0:T(4,128)(2,1)} %res_ref.1, f32[5376]{0:T(1024)} %gain_ref.1, bf16[256,5376]{1,0:T(8,128)(2,1)} %w_hbm.1), custom_call_target="tpu_custom_call" | custom-call | flops 2147483648 | bytes 16777216 | tf_op jit(solution)/shard_map/pallas_call | solution.py:427
  45.1 1.5 %copy.8 = f32[4,5376]{1,0:T(4,128)} copy(f32[4,5376]{1,0:T(4,128)} %shard_map.64) | data formatting | bytes 172032

commit v6 on v5

--- a/solution.py
+++ b/solution.py
@@ -98,12 +98,16 @@
 
     w_copy = pltpu.make_async_copy(w_hbm, w_buf, w_sem)
 
-    @pl.loop(0, kv_heads)
-    def _(step):
+    def load(step):
         k_copy(head_at(step)).start()
         v_copy(head_at(step)).start()
 
-    w_copy.start()
+    first_loads = min(3, kv_heads)
+    ahead = min(first_loads + 3, kv_heads)
+
+    @pl.loop(0, first_loads)
+    def _(step):
+        load(step)
 
     barrier = pltpu.get_barrier_semaphore()
 
@@ -145,6 +149,10 @@
 
     q_copy(me, across, 0).start()
     q_copy(me, sibling, depth).start()
+
+    @pl.loop(first_loads, ahead)
+    def _(step):
+        load(step)
 
     @pl.loop(1, depth)
     def _(step):
@@ -213,6 +221,14 @@
 
     @pl.loop(0, kv_heads)
     def _(step):
+        @pl.when(step + ahead < kv_heads)
+        def _():
+            load(step + ahead)
+
+        @pl.when(step == kv_heads // 2)
+        def _():
+            w_copy.start()
+
         h = head_at(step)
         rank = lax.rem(step, chips)
         its_z, its_y = place_at(rank)

time: 46.9 us -> 46.8 us (level)
  no operation moved by 1% of the time
where the time goes in v6:
time: 46.8 us; the launch traced here: 46.6 us
  Pallas kernels  45.1 us (96%)
  local copies, waits for them, and re-layouts  1.53 us (3%)
    pallas_call x1, Pallas kernels, shards(): pl.pallas_call(functools.partial(kernel, n, group_size), out_shape=jax.Sh...  45.1 us
    unnamed x1, local copies, waits for them, and re-layouts  1.53 us

profile of v6, /device:TPU:0, one launch (start us, length us, event | category | flops | bytes accessed | tf_op | source)
XLA Modules:
  0.0 46.6 jit_solution(11871744936756836767)
XLA Ops:
  0.0 45.1 %shard_map.64 = f32[4,5376]{1,0:T(4,128)} custom-call(bf16[4,4096]{1,0:T(4,128)(2,1)} %q_ref.1, bf16[16,2048,128]{2,1,0:T(8,128)(2,1)} %k_hbm.1, bf16[16,2048,128]{2,1,0:T(8,128)(2,1)} %v_hbm.1, bf16[4,5376]{1,0:T(4,128)(2,1)} %res_ref.1, f32[5376]{0:T(1024)} %gain_ref.1, bf16[256,5376]{1,0:T(8,128)(2,1)} %w_hbm.1), custom_call_target="tpu_custom_call" | custom-call | flops 2147483648 | bytes 16777216 | tf_op jit(solution)/shard_map/pallas_call | solution.py:443
  45.1 1.5 %copy.8 = f32[4,5376]{1,0:T(4,128)} copy(f32[4,5376]{1,0:T(4,128)} %shard_map.64) | data formatting | bytes 172032

commit v7 on v6

--- a/solution.py
+++ b/solution.py
@@ -299,14 +299,19 @@
     _, total, weighted = merge([get(deep_got, i) for i in range(depth)])
     attended = (weighted / total).astype(bf16)
 
-    unit = lax.broadcasted_iota(jnp.int32, (units, rows), 0)
-    column = lax.broadcasted_iota(jnp.int32, (units, rows), 1)
+    folds = y_out.shape[3] // (depth * own_units)
+    tall = own_units * folds
+    out_rows = n * tall
+    row = lax.broadcasted_iota(jnp.int32, (out_rows, rows), 0)
+    column = lax.broadcasted_iota(jnp.int32, (out_rows, rows), 1)
+    block = lax.div(row, tall)
+    owner = device(
+        lax.rem(block, depth), lax.rem(lax.div(block, depth), 2), lax.div(block, 2 * depth)
+    )
     first = lax.rem(me, owners) * own_heads
     blocks = []
     for g in range(own_heads):
-        place = (
-            lax.div(unit, own_units) * own_rows + (first + g) * own_units + lax.rem(unit, own_units)
-        )
+        place = owner * own_rows + (first + g) * own_units + lax.rem(row, own_units)
         pick = jnp.where(column == place, 1.0, 0.0).astype(bf16)
         blocks.append(
             lax.dot_general(
@@ -349,14 +354,19 @@
 
     chunks = y_out.shape[0]
     cols = y_out.shape[-1]
+    stretch = width // folds
+    fold = lax.rem(
+        lax.div(lax.broadcasted_iota(jnp.int32, (out_rows, cols), 0), own_units), folds
+    )
     for c in range(chunks):
-        product = jnp.dot(
-            own_block, w_buf[:, c * cols : (c + 1) * cols], preferred_element_type=f32
-        )
-        for k in range(n):
-            y_out[c, k % 2, k // 2 % 2, k // 4] = product[
-                k * own_units : (k + 1) * own_units
-            ].astype(bf16)
+        product = None
+        for part in range(folds):
+            at_part = part * stretch + c * cols
+            term = jnp.dot(
+                own_block, w_buf[:, at_part : at_part + cols], preferred_element_type=f32
+            )
+            product = term if product is None else jnp.where(fold == part, term, product)
+        y_out[c] = product.astype(bf16).reshape(2, 2, depth * tall, cols)
         core_copy(c).start()
     for c in range(chunks):
         core_copy(c).wait_recv()
@@ -367,7 +377,8 @@
     for c in range(chunks):
         own_sum = y_out[c, core, y].astype(f32) + core_in[c, y].astype(f32)
         across_copy(c).wait_recv()
-        z_out[c] = (own_sum + across_in[c].astype(f32)).astype(bf16)
+        own_sum = (own_sum + across_in[c].astype(f32)).reshape(depth, tall, cols)
+        z_out[c] = own_sum.astype(bf16)
 
         @pl.loop(1, depth)
         def _(step):
@@ -383,11 +394,14 @@
 
         branches.append(jnp.sum(z_in[c].astype(f32), axis=0))
     squares = sum(jnp.sum(b * b, axis=1, keepdims=True) for b in branches)
+    squares = sum(squares[p * own_units : (p + 1) * own_units] for p in range(folds))
     inverse = lax.rsqrt(squares / width + 1e-06)
     for c, branch in enumerate(branches):
-        span = pl.ds(c * cols, cols)
-        gain = gain_ref[span].reshape(1, cols)
-        out_ref[:, span] = res_ref[:, span].astype(f32) + branch * inverse * gain
+        for p in range(folds):
+            span = pl.ds(p * stretch + c * cols, cols)
+            gain = gain_ref[span].reshape(1, cols)
+            mine = branch[p * own_units : (p + 1) * own_units]
+            out_ref[:, span] = res_ref[:, span].astype(f32) + mine * inverse * gain
 
     @pl.loop(0, n)
     def _(step):
@@ -427,8 +441,10 @@
     own_rows = own_units * group_size
     rows = n * own_rows
     width = residual.shape[1]
-    cols = chunk_of(width, 2048)
-    chunks = width // cols
+    folds = max(1, 8 // own_units)
+    tall = own_units * folds
+    cols = chunk_of(width // folds, 1024)
+    chunks = width // folds // cols
     depth = n // 4
     vmem = pl.BlockSpec(memory_space=pltpu.VMEM)
     hbm = pl.BlockSpec(memory_space=pl.ANY)
@@ -458,12 +474,12 @@
             partials(depth),
             pltpu.VMEM((head_dim, rows), f32),
             pltpu.VMEM((8, rows), f32),
-            pltpu.VMEM((chunks, 2, 2, depth, own_units, cols), bf16),
-            pltpu.VMEM((chunks, 2, depth, own_units, cols), bf16),
-            pltpu.VMEM((chunks, depth, own_units, cols), bf16),
-            pltpu.VMEM((chunks, depth, own_units, cols), bf16),
-            pltpu.VMEM((chunks, depth, own_units, cols), bf16),
-            pltpu.VMEM((chunks, depth, own_units, cols), bf16),
+            pltpu.VMEM((chunks, 2, 2, depth * tall, cols), bf16),
+            pltpu.VMEM((chunks, 2, depth * tall, cols), bf16),
+            pltpu.VMEM((chunks, depth * tall, cols), bf16),
+            pltpu.VMEM((chunks, depth * tall, cols), bf16),
+            pltpu.VMEM((chunks, depth, tall, cols), bf16),
+            pltpu.VMEM((chunks, depth, tall, cols), bf16),
             dma((kv_heads,)),
             dma((kv_heads,)),
             dma,

time: 46.8 us -> 46.9 us (level)
  no operation moved by 1% of the time
where the time goes in v7:
time: 46.9 us; the launch traced here: 46.7 us
  Pallas kernels  45.1 us (96%)
  local copies, waits for them, and re-layouts  1.53 us (3%)
    pallas_call x1, Pallas kernels, shards(): pl.pallas_call(functools.partial(kernel, n, group_size), out_shape=jax.Sh...  45.1 us
    unnamed x1, local copies, waits for them, and re-layouts  1.53 us

profile of v7, /device:TPU:0, one launch (start us, length us, event | category | flops | bytes accessed | tf_op | source)
XLA Modules:
  0.0 46.7 jit_solution(7285648267839293767)
XLA Ops:
  0.0 45.1 %shard_map.64 = f32[4,5376]{1,0:T(4,128)} custom-call(bf16[4,4096]{1,0:T(4,128)(2,1)} %q_ref.1, bf16[16,2048,128]{2,1,0:T(8,128)(2,1)} %k_hbm.1, bf16[16,2048,128]{2,1,0:T(8,128)(2,1)} %v_hbm.1, bf16[4,5376]{1,0:T(4,128)(2,1)} %res_ref.1, f32[5376]{0:T(1024)} %gain_ref.1, bf16[256,5376]{1,0:T(8,128)(2,1)} %w_hbm.1), custom_call_target="tpu_custom_call" | custom-call | flops 2147483648 | bytes 16777216 | tf_op jit(solution)/shard_map/pallas_call | solution.py:459
  45.2 1.5 %copy.8 = f32[4,5376]{1,0:T(4,128)} copy(f32[4,5376]{1,0:T(4,128)} %shard_map.64) | data formatting | bytes 172032

commit v8 on v6

--- a/solution.py
+++ b/solution.py
@@ -1,5 +1,4 @@
 import functools
-import math
 
 import jax
 import jax.numpy as jnp
@@ -75,7 +74,7 @@
     rows = n * own_rows
     units = n * own_units
     width = w_buf.shape[1]
-    scale = 168.0**-0.5 * math.log2(math.e)
+    scale = 168.0**-0.5
     chips = n // 2
 
     def place_at(rank):
@@ -213,7 +212,7 @@
 
     def merge(partials):
         peak = functools.reduce(jnp.maximum, [p for p, _, _ in partials])
-        factors = [jnp.exp2(p - peak) for p, _, _ in partials]
+        factors = [jnp.exp(p - peak) for p, _, _ in partials]
         total = sum(f * t for f, (_, t, _) in zip(factors, partials))
         return peak, total, sum(f * w for f, (_, _, w) in zip(factors, partials))
 
@@ -245,7 +244,7 @@
                 preferred_element_type=f32,
             )
             peak = jnp.max(scores, axis=0, keepdims=True) * scale
-            exponent = jnp.exp2(scores * scale - peak)
+            exponent = jnp.exp(scores * scale - peak)
             total = jnp.sum(exponent, axis=0, keepdims=True)
             weighted = lax.dot_general(
                 v_buf[h, pl.ds(t, tile), :],

time: 46.8 us -> 47 us (level)
  no operation moved by 1% of the time
where the time goes in v8:
time: 47 us; the launch traced here: 46.8 us
  Pallas kernels  45.3 us (96%)
  local copies, waits for them, and re-layouts  1.53 us (3%)
    pallas_call x1, Pallas kernels, shards(): pl.pallas_call(functools.partial(kernel, n, group_size), out_shape=jax.Sh...  45.3 us
    unnamed x1, local copies, waits for them, and re-layouts  1.53 us

profile of v8, /device:TPU:0, one launch (start us, length us, event | category | flops | bytes accessed | tf_op | source)
XLA Modules:
  0.0 46.8 jit_solution(12054374591294054208)
XLA Ops:
  0.0 45.3 %shard_map.64 = f32[4,5376]{1,0:T(4,128)} custom-call(bf16[4,4096]{1,0:T(4,128)(2,1)} %q_ref.1, bf16[16,2048,128]{2,1,0:T(8,128)(2,1)} %k_hbm.1, bf16[16,2048,128]{2,1,0:T(8,128)(2,1)} %v_hbm.1, bf16[4,5376]{1,0:T(4,128)(2,1)} %res_ref.1, f32[5376]{0:T(1024)} %gain_ref.1, bf16[256,5376]{1,0:T(8,128)(2,1)} %w_hbm.1), custom_call_target="tpu_custom_call" | custom-call | flops 2147483648 | bytes 16777216 | tf_op jit(solution)/shard_map/pallas_call | solution.py:442
  45.3 1.5 %copy.8 = f32[4,5376]{1,0:T(4,128)} copy(f32[4,5376]{1,0:T(4,128)} %shard_map.64) | data formatting | bytes 172032

commit v9 on v6

--- a/solution.py
+++ b/solution.py
@@ -219,27 +219,67 @@
 
     tile = chunk_of(context, 512)
 
-    @pl.loop(0, kv_heads)
-    def _(step):
-        @pl.when(step + ahead < kv_heads)
-        def _():
-            load(step + ahead)
-
-        @pl.when(step == kv_heads // 2)
-        def _():
-            w_copy.start()
-
-        h = head_at(step)
+    def exchange(i, step):
         rank = lax.rem(step, chips)
         its_z, its_y = place_at(rank)
         chip = its_z * 2 + its_y
-        q = q_all[:, h].astype(f32).reshape(rows, head_dim).astype(bf16)
-        k_copy(h).wait()
-        v_copy(h).wait()
-        partials = []
+
+        def mine():
+            return mine_stat[i, 0:1, :], mine_stat[i, 1:2, :], mine_weighted[i]
+
+        @pl.when((step < chips) if owners == 1 else (step >= 0))
+        def _():
+            put(core_out, chip, mine())
+            start(to_core(chip))
+
+        @pl.when((step >= chips) if owners == 1 else (step >= 0))
+        def _():
+            for copy in to_core(chip):
+                copy.wait_recv()
+            two = merge([mine(), get(core_got, chip)])
+
+            @pl.when(rank < depth)
+            def _():
+                put(cross_out, its_z, two)
+                start(to_across(its_z))
+
+            @pl.when(rank >= depth)
+            def _():
+                for copy in to_across(its_z):
+                    copy.wait_recv()
+                put(deep_out, its_z, merge([two, get(cross_got, its_z)]))
+
+                @pl.when(its_z != z)
+                def _():
+                    start(to_z(its_z, z))
+
+    @pl.loop(0, kv_heads // 2)
+    def _(pair):
+        steps = [2 * pair, 2 * pair + 1]
+        heads = [head_at(step) for step in steps]
+        for step in steps:
+
+            @pl.when(step + ahead < kv_heads)
+            def _():
+                load(step + ahead)
+
+        @pl.when(pair == kv_heads // 4)
+        def _():
+            w_copy.start()
+
+        empty = jnp.zeros((rows, head_dim), bf16)
+        q0, q1 = [q_all[:, h].astype(f32).reshape(rows, head_dim).astype(bf16) for h in heads]
+        q = jnp.concatenate(
+            [jnp.concatenate([q0, empty], axis=1), jnp.concatenate([empty, q1], axis=1)], axis=0
+        )
+        for h in heads:
+            k_copy(h).wait()
+            v_copy(h).wait()
+        partials = [[], []]
         for t in range(0, context, tile):
+            span = pl.ds(t, tile)
             scores = lax.dot_general(
-                k_buf[h, pl.ds(t, tile), :],
+                jnp.concatenate([k_buf[h, span, :] for h in heads], axis=1),
                 q,
                 (((1,), (1,)), ((), ())),
                 preferred_element_type=f32,
@@ -247,46 +287,23 @@
             peak = jnp.max(scores, axis=0, keepdims=True) * scale
             exponent = jnp.exp2(scores * scale - peak)
             total = jnp.sum(exponent, axis=0, keepdims=True)
-            weighted = lax.dot_general(
-                v_buf[h, pl.ds(t, tile), :],
-                exponent.astype(bf16),
-                (((0,), (0,)), ((), ())),
-                preferred_element_type=f32,
-            )
-            partials.append((peak, total, weighted))
-        peak, total, weighted = merge(partials)
-        mine_weighted[...] = weighted
-        mine_stat[0:1, :] = peak
-        mine_stat[1:2, :] = total
-
-        def mine():
-            return mine_stat[0:1, :], mine_stat[1:2, :], mine_weighted[...]
-
-        @pl.when((step < chips) if owners == 1 else (step >= 0))
-        def _():
-            put(core_out, chip, mine())
-            start(to_core(chip))
-
-        @pl.when((step >= chips) if owners == 1 else (step >= 0))
-        def _():
-            for copy in to_core(chip):
-                copy.wait_recv()
-            two = merge([mine(), get(core_got, chip)])
-
-            @pl.when(rank < depth)
-            def _():
-                put(cross_out, its_z, two)
-                start(to_across(its_z))
-
-            @pl.when(rank >= depth)
-            def _():
-                for copy in to_across(its_z):
-                    copy.wait_recv()
-                put(deep_out, its_z, merge([two, get(cross_got, its_z)]))
-
-                @pl.when(its_z != z)
-                def _():
-                    start(to_z(its_z, z))
+            weights = exponent.astype(bf16)
+            for i, h in enumerate(heads):
+                half = slice(i * rows, (i + 1) * rows)
+                weighted = lax.dot_general(
+                    v_buf[h, span, :],
+                    weights[:, half],
+                    (((0,), (0,)), ((), ())),
+                    preferred_element_type=f32,
+                )
+                partials[i].append((peak[:, half], total[:, half], weighted))
+        for i in range(2):
+            peak, total, weighted = merge(partials[i])
+            mine_weighted[i] = weighted
+            mine_stat[i, 0:1, :] = peak
+            mine_stat[i, 1:2, :] = total
+        for i, step in enumerate(steps):
+            exchange(i, step)
 
     deep_got[0][z] = deep_out[0][z]
     deep_got[1][z] = deep_out[1][z]
@@ -456,8 +473,8 @@
             partials(depth),
             partials(depth),
             partials(depth),
-            pltpu.VMEM((head_dim, rows), f32),
-            pltpu.VMEM((8, rows), f32),
+            pltpu.VMEM((2, head_dim, rows), f32),
+            pltpu.VMEM((2, 8, rows), f32),
             pltpu.VMEM((chunks, 2, 2, depth, own_units, cols), bf16),
             pltpu.VMEM((chunks, 2, depth, own_units, cols), bf16),
             pltpu.VMEM((chunks, depth, own_units, cols), bf16),

time: 46.8 us -> 46.1 us (0.985)
  Pallas kernels: 45.1 us -> 44.3 us
    pallas_call x1, Pallas kernels: 45.1 us -> 44.3 us  [shards(): pl.pallas_call(functools.partial(kernel, n, group_size), out_shape=jax.Sh...]
where the time goes in v9:
time: 46.1 us; the launch traced here: 45.9 us
  Pallas kernels  44.3 us (96%)
  local copies, waits for them, and re-layouts  1.53 us (3%)
    pallas_call x1, Pallas kernels, shards(): pl.pallas_call(functools.partial(kernel, n, group_size), out_shape=jax.Sh...  44.3 us
    unnamed x1, local copies, waits for them, and re-layouts  1.53 us

profile of v9, /device:TPU:0, one launch (start us, length us, event | category | flops | bytes accessed | tf_op | source)
XLA Modules:
  0.0 45.9 jit_solution(1055350067827979191)
XLA Ops:
  0.0 44.3 %shard_map.64 = f32[4,5376]{1,0:T(4,128)} custom-call(bf16[4,4096]{1,0:T(4,128)(2,1)} %q_ref.1, bf16[16,2048,128]{2,1,0:T(8,128)(2,1)} %k_hbm.1, bf16[16,2048,128]{2,1,0:T(8,128)(2,1)} %v_hbm.1, bf16[4,5376]{1,0:T(4,128)(2,1)} %res_ref.1, f32[5376]{0:T(1024)} %gain_ref.1, bf16[256,5376]{1,0:T(8,128)(2,1)} %w_hbm.1), custom_call_target="tpu_custom_call" | custom-call | flops 2147483648 | bytes 16777216 | tf_op jit(solution)/shard_map/pallas_call | solution.py:460
  44.4 1.5 %copy.8 = f32[4,5376]{1,0:T(4,128)} copy(f32[4,5376]{1,0:T(4,128)} %shard_map.64) | data formatting | bytes 172032

commit v10 on v9

--- a/solution.py
+++ b/solution.py
@@ -28,6 +28,7 @@
     out_ref,
     k_buf,
     v_buf,
+    v_turned,
     w_buf,
     q_all,
     core_out,
@@ -100,14 +101,19 @@
 
     def load(step):
         k_copy(head_at(step)).start()
+
+    ahead = min(6, kv_heads)
+
+    @pl.loop(0, kv_heads)
+    def _(step):
         v_copy(head_at(step)).start()
 
-    first_loads = min(3, kv_heads)
-    ahead = min(first_loads + 3, kv_heads)
-
-    @pl.loop(0, first_loads)
-    def _(step):
-        load(step)
+    def turn(begin, end):
+        @pl.loop(begin, end)
+        def _(step):
+            h = head_at(step)
+            v_copy(h).wait()
+            v_turned[h] = v_buf[h].T
 
     barrier = pltpu.get_barrier_semaphore()
 
@@ -150,9 +156,12 @@
     q_copy(me, across, 0).start()
     q_copy(me, sibling, depth).start()
 
-    @pl.loop(first_loads, ahead)
+    @pl.loop(0, ahead)
     def _(step):
         load(step)
+
+    third = kv_heads // 3
+    turn(0, third)
 
     @pl.loop(1, depth)
     def _(step):
@@ -161,11 +170,15 @@
         q_copy(source, across, 2 * depth + step).start()
         q_copy(source, sibling, depth + step).start()
 
+    turn(third, 2 * third)
+
     @pl.loop(0, depth)
     def _(step):
         source = at_z(depth - step, 1 - y)
         q_copy(source, sibling, 0).wait_recv()
         q_copy(source, sibling, 3 * depth + step).start()
+
+    turn(2 * third, kv_heads)
 
     @pl.loop(0, n // 2)
     def _(step):
@@ -274,7 +287,6 @@
         )
         for h in heads:
             k_copy(h).wait()
-            v_copy(h).wait()
         partials = [[], []]
         for t in range(0, context, tile):
             span = pl.ds(t, tile)
@@ -290,11 +302,8 @@
             weights = exponent.astype(bf16)
             for i, h in enumerate(heads):
                 half = slice(i * rows, (i + 1) * rows)
-                weighted = lax.dot_general(
-                    v_buf[h, span, :],
-                    weights[:, half],
-                    (((0,), (0,)), ((), ())),
-                    preferred_element_type=f32,
+                weighted = jnp.dot(
+                    v_turned[h, :, span], weights[:, half], preferred_element_type=f32
                 )
                 partials[i].append((peak[:, half], total[:, half], weighted))
         for i in range(2):
@@ -465,6 +474,7 @@
         scratch_shapes=[
             pltpu.VMEM(keys.shape, bf16),
             pltpu.VMEM(values.shape, bf16),
+            pltpu.VMEM((kv_heads, head_dim, context), bf16),
             pltpu.VMEM(out_weight.shape, bf16),
             pltpu.VMEM((n, kv_heads, own_rows, head_dim), bf16),
             partials(n // 2),

time: 46.1 us -> 46.9 us (1.017)
  Pallas kernels: 44.3 us -> 45.1 us
    pallas_call x1, Pallas kernels: 44.3 us -> 45.1 us  [shards(): pl.pallas_call(functools.partial(kernel, n, group_size), out_shape=jax.Sh...]
where the time goes in v10:
time: 46.9 us; the launch traced here: 46.7 us
  Pallas kernels  45.1 us (96%)
  local copies, waits for them, and re-layouts  1.53 us (3%)
    pallas_call x1, Pallas kernels, shards(): pl.pallas_call(functools.partial(kernel, n, group_size), out_shape=jax.Sh...  45.1 us
    unnamed x1, local copies, waits for them, and re-layouts  1.53 us

profile of v10, /device:TPU:0, one launch (start us, length us, event | category | flops | bytes accessed | tf_op | source)
XLA Modules:
  0.0 46.7 jit_solution(13966424775557280451)
XLA Ops:
  0.0 45.1 %shard_map.64 = f32[4,5376]{1,0:T(4,128)} custom-call(bf16[4,4096]{1,0:T(4,128)(2,1)} %q_ref.1, bf16[16,2048,128]{2,1,0:T(8,128)(2,1)} %k_hbm.1, bf16[16,2048,128]{2,1,0:T(8,128)(2,1)} %v_hbm.1, bf16[4,5376]{1,0:T(4,128)(2,1)} %res_ref.1, f32[5376]{0:T(1024)} %gain_ref.1, bf16[256,5376]{1,0:T(8,128)(2,1)} %w_hbm.1), custom_call_target="tpu_custom_call" | custom-call | flops 2147483648 | bytes 16777216 | tf_op jit(solution)/shard_map/pallas_call | solution.py:469
  45.1 1.5 %copy.8 = f32[4,5376]{1,0:T(4,128)} copy(f32[4,5376]{1,0:T(4,128)} %shard_map.64) | data formatting | bytes 172032

commit v11 on v9

--- a/solution.py
+++ b/solution.py
@@ -444,7 +444,7 @@
     own_rows = own_units * group_size
     rows = n * own_rows
     width = residual.shape[1]
-    cols = chunk_of(width, 2048)
+    cols = chunk_of(width, 2688)
     chunks = width // cols
     depth = n // 4
     vmem = pl.BlockSpec(memory_space=pltpu.VMEM)

time: 46.1 us -> 46 us (level)
  no operation moved by 1% of the time
where the time goes in v11:
time: 46 us; the launch traced here: 45.8 us
  Pallas kernels  44.3 us (96%)
  local copies, waits for them, and re-layouts  1.53 us (3%)
    pallas_call x1, Pallas kernels, shards(): pl.pallas_call(functools.partial(kernel, n, group_size), out_shape=jax.Sh...  44.3 us
    unnamed x1, local copies, waits for them, and re-layouts  1.53 us

profile of v11, /device:TPU:0, one launch (start us, length us, event | category | flops | bytes accessed | tf_op | source)
XLA Modules:
  0.0 45.8 jit_solution(2354433396454295956)
XLA Ops:
  0.0 44.3 %shard_map.64 = f32[4,5376]{1,0:T(4,128)} custom-call(bf16[4,4096]{1,0:T(4,128)(2,1)} %q_ref.1, bf16[16,2048,128]{2,1,0:T(8,128)(2,1)} %k_hbm.1, bf16[16,2048,128]{2,1,0:T(8,128)(2,1)} %v_hbm.1, bf16[4,5376]{1,0:T(4,128)(2,1)} %res_ref.1, f32[5376]{0:T(1024)} %gain_ref.1, bf16[256,5376]{1,0:T(8,128)(2,1)} %w_hbm.1), custom_call_target="tpu_custom_call" | custom-call | flops 2147483648 | bytes 16777216 | tf_op jit(solution)/shard_map/pallas_call | solution.py:460
  44.3 1.5 %copy.8 = f32[4,5376]{1,0:T(4,128)} copy(f32[4,5376]{1,0:T(4,128)} %shard_map.64) | data formatting | bytes 172032
